TPU v7x, 32 devices: a whole 2x2x4 slice. The times are simulated.
32 devices in a mesh: grp: 2 (over x), tmpl: 8 (over z, y), tm: 2 (over core).
Axes of the slice: x: 2, y: 2, z: 4, core: 2. Of those that a mesh axis runs over, the one named last changes fastest.
Arguments:
- spectra: bfloat16 [1024, 4, 8192], P(('grp', 'tm', 'tmpl')), parts along dimension 0, may hold values from -6 to 6
- offsets: int32 [1024, 16], P(('grp', 'tm'), 'tmpl'), parts along dimension 0, may hold values from 0 to 1008
- fractions: float32 [4096], P(('grp', 'tmpl')), parts along dimension 0, may hold values from 0.1 to 0.9
- antenna: float32 [1024, 4], P('grp'), parts along dimension 0, may hold values from -2 to 2, as said below
- starts: int32 [64], P('grp'), parts along dimension 0, may hold values from 0 to 255
- durations: int32 [64], P('grp'), parts along dimension 0, may hold values from 48 to 256
Outputs:
- fstat_map: float32 [32, 32, 4096], P('tm', None, ('grp', 'tmpl')), parts along dimension 2
- loudest: float32 [64, 32], P(('grp', 'tm')), parts along dimension 0
There are 2 independent parts, one for each index of `grp`. A program takes and returns all parts, laid end to end along the dimension named above; each array names one. Nothing has to cross between parts.
Inputs may be any that keep to these rules, and one draw needn't show every extreme that they name: `antenna`: each detector's responses a and b turn once every 48 SFTs with magnitudes that vary from SFT to SFT.
All inputs are finite; a program needn't handle non-finite values.
Results may differ from a plain program's by a relative error of at most 0.0051.
Values may be sent and summed in bfloat16 or wider, within the bound.
No kernel may reach another device: no remote copies, remote signals or barrier semaphores. Data moves between devices by JAX's collectives and lax.ppermute only.
A program may use at most 128 MiB of HBM per device.

v0:
```python
import functools

import jax
import jax.numpy as jnp
from jax import lax
from jax.experimental import pallas as pl
from jax.experimental.pallas import tpu as pltpu
from jax.sharding import PartitionSpec as P

W = 16
LANES = 128
NT = (((1,), (1,)), ((), ()))


def iota(shape, axis):
    return lax.broadcasted_iota(jnp.int32, shape, axis)


def order(size, first):
    members = list(range(size))
    members[0], members[first] = first, 0
    return members


def hold_kernel(spec_ref, out_ref, sem):
    copy = pltpu.make_async_copy(spec_ref, out_ref, sem)
    copy.start()
    copy.wait()


def hold(spectra):
    return pl.pallas_call(
        hold_kernel,
        out_shape=jax.ShapeDtypeStruct(spectra.shape, spectra.dtype),
        in_specs=[pl.BlockSpec(memory_space=pl.ANY)],
        out_specs=pl.BlockSpec(memory_space=pltpu.VMEM),
        scratch_shapes=[pltpu.SemaphoreType.DMA],
        compiler_params=pltpu.CompilerParams(vmem_limit_bytes=8 * 1024 * 1024),
        cost_estimate=pl.CostEstimate(flops=0, bytes_accessed=4 * spectra.size, transcendentals=0),
        name="hold",
    )(spectra)


def pick_kernel(bands_in, bands_out, me_ref, offset_ref, spec_ref, out_ref, place_ref, turn_ref, tile_ref, sem):
    rows, _, bins = spec_ref.shape
    bands, blocks, _ = offset_ref.shape
    band_width = bins // bands
    groups = rows // 8
    chunks = band_width // LANES
    width = blocks * W
    first = me_ref[0] * rows
    columns = pl.ds(pl.multiple_of(first // LANES * LANES, LANES), LANES)
    offsets = jnp.concatenate([offset_ref[bands_in.index(band), :, columns] for band in range(bands)], axis=0).astype(jnp.float32)
    lane = iota(offsets.shape, 1)
    offsets = jnp.take_along_axis(offsets, (lane >> 2) + first & (LANES - 1), axis=1, mode="promise_in_bounds")
    offsets = jnp.concatenate([offsets, jnp.zeros((LANES - bands * blocks, LANES), jnp.float32)], axis=0)
    upright = jnp.transpose(offsets).astype(jnp.int32)
    lane = iota((32, LANES), 1)
    places = upright[0:32]
    for group in range(1, groups):
        turned = pltpu.roll(upright[group * 32 : group * 32 + 32], group * bands * blocks, 1)
        places = jnp.where(lane < group * bands * blocks, places, turned)
    lane = iota((8, LANES), 1)
    lane_group = lane // width
    source = lane_group * (bands * blocks) + lane // W % blocks
    for band in range(bands):
        for pair in range(4):
            place = jnp.take_along_axis(places[pair * 8 : pair * 8 + 8], source + band * blocks, axis=1, mode="promise_in_bounds")
            place_ref[band, pair] = place + ((lane & (W - 1)) + lane_group * band_width)

    def step(band, carry):
        for pair in range(4):
            place = place_ref[band, pair]
            lane_id = place & (LANES - 1)
            chosen = place >> 7
            tile = jnp.zeros((8, LANES), jnp.float32)
            for group in range(groups):
                for chunk in range(chunks):
                    start = pl.multiple_of(band * band_width + chunk * LANES, LANES)
                    values = spec_ref[pl.ds(group * 8 + pair * 2, 2), :, pl.ds(start, LANES)]
                    values = values.astype(jnp.float32).reshape(8, LANES)
                    moved = jnp.take_along_axis(values, lane_id, axis=1, mode="promise_in_bounds")
                    tile = jnp.where(chosen == group * chunks + chunk, moved, tile)
            turn_ref[band, pl.ds(pair * 8, 8), :] = tile
        return carry

    lax.fori_loop(0, bands, step, 0)
    tiles = {}
    for band in range(bands):
        parts = [turn_ref[band, pl.ds(part, 8, stride=4), :] for part in range(4)]
        for group in range(groups):
            tile = jnp.zeros((8, LANES), jnp.float32)
            for part in range(4):
                amount = (part - group) * width % LANES
                turned = pltpu.roll(parts[part], amount, 1) if amount else parts[part]
                tile = jnp.where(lane_group == part, turned, tile)
            tiles[band, group] = tile
    wanted = [tiles[band, group] for band in bands_out for group in range(groups)]
    for n in range(0, len(wanted), 2):
        tile_ref[n * 8 : n * 8 + 16, :] = jnp.concatenate(wanted[n : n + 2], axis=0).astype(jnp.bfloat16)
    copy = pltpu.make_async_copy(tile_ref, out_ref, sem)
    copy.start()
    copy.wait()


def pick(me, offsets, spectra, bands_in, bands_out):
    rows, bands = spectra.shape[0], offsets.shape[0]
    out_rows = len(bands_out) * rows
    vmem = pl.BlockSpec(memory_space=pltpu.VMEM)
    return pl.pallas_call(
        functools.partial(pick_kernel, bands_in, bands_out),
        out_shape=jax.ShapeDtypeStruct((out_rows, LANES), jnp.bfloat16),
        in_specs=[pl.BlockSpec(memory_space=pltpu.SMEM), vmem, vmem],
        out_specs=pl.BlockSpec(memory_space=pl.ANY),
        scratch_shapes=[
            pltpu.VMEM((bands, 4, 8, LANES), jnp.int32),
            pltpu.VMEM((bands, 32, LANES), jnp.float32),
            pltpu.VMEM((out_rows, LANES), jnp.bfloat16),
            pltpu.SemaphoreType.DMA,
        ],
        compiler_params=pltpu.CompilerParams(vmem_limit_bytes=8 * 1024 * 1024),
        cost_estimate=pl.CostEstimate(flops=10_000_000, bytes_accessed=2 * spectra.size, transcendentals=0),
        name="pick",
    )(me, offsets, spectra)


def split(values, count):
    parts = []
    for _ in range(count):
        part = values.astype(jnp.bfloat16)
        parts.append(part)
        values = values - part.astype(jnp.float32)
    return parts


def prepare_kernel(first, run, durations_ref, starts_ref, antenna_ref, fractions_ref, mask_ref, weigh_ref, coef_ref, kernel_ref):
    rows = starts_ref.shape[0]
    count = durations_ref.shape[0]
    sfts = antenna_ref.shape[1]
    sft = iota((rows, sfts), 1)
    sft = jnp.where(sft // run == 0, sft + first * run, jnp.where(sft // run == first, sft - first * run, sft))
    start = starts_ref[:, 0:1]
    after = sft >= start
    for j in range(count):
        inside = after & (sft < start + durations_ref[j])
        mask_ref[pl.ds(j * rows, rows), :] = jnp.where(inside, 1.0, 0.0).astype(jnp.bfloat16)
    antenna = jnp.concatenate([antenna_ref[...], jnp.zeros((4, sfts), jnp.float32)], axis=0)
    place = iota(antenna.shape, 1) // run
    after = pltpu.roll(antenna, sfts - first * run, 1)
    before = pltpu.roll(antenna, first * run, 1)
    antenna = jnp.where(place == 0, after, jnp.where(place == first, before, antenna))
    a1, a2, b1, b2 = (antenna[n : n + 1] for n in range(4))
    terms = jnp.concatenate([a1 * a1 + a2 * a2, b1 * b1 + b2 * b2, a1 * b1 + a2 * b2, jnp.zeros((5, sfts), jnp.float32)], axis=0)
    weights = sum(lax.dot_general(mask_ref[...], part, NT, preferred_element_type=jnp.float32) for part in split(terms, 3))
    wa, wb, wc = (weights[:, n : n + 1] for n in range(3))
    shape = (rows * count, LANES)
    late = iota(shape, 1) >= LANES // 2
    coef_ref[0] = jnp.broadcast_to(1.0 / wa, shape)
    coef_ref[1] = jnp.broadcast_to(wa / (wa * wb - wc * wc), shape)
    coef_ref[2] = jnp.where(late, jnp.broadcast_to(wc / wa, shape), 0.0)
    upright = jnp.transpose(jnp.concatenate([antenna, jnp.zeros((LANES - 8, sfts), jnp.float32)], axis=0))
    shape = (sfts, LANES)
    late = iota(shape, 1) >= LANES // 2
    weigh_ref[0] = jnp.where(late, upright[:, 3:4], upright[:, 0:1])
    weigh_ref[1] = jnp.where(late, upright[:, 2:3], upright[:, 1:2])
    fractions = fractions_ref[...]
    templates = fractions.shape[1]
    blocks = kernel_ref.shape[1] // (4 * LANES)
    bin_id = iota((W, templates), 0)
    distance = fractions + (W // 2 - 1) - bin_id.astype(jnp.float32)
    alternate = 1.0 - 2.0 * (bin_id % 2).astype(jnp.float32)
    values = (alternate * jnp.sin(jnp.pi * fractions) / (jnp.pi * distance)).astype(jnp.bfloat16)
    kernel_ref[...] = jnp.zeros_like(kernel_ref)
    for part in range(2):
        for c in range(4):
            for b in range(blocks):
                row = ((part * 4 + c) * blocks + b) * W
                column = (c * blocks + b) * LANES
                kernel_ref[pl.ds(row, W), pl.ds(column, LANES)] = values[:, b * LANES : (b + 1) * LANES]


def prepare(durations, starts, antenna, fractions, first, run):
    count, rows, sfts = durations.shape[0], starts.shape[0], antenna.shape[0]
    columns = 4 * fractions.shape[0]
    features = 4 * W * (fractions.shape[0] // LANES)
    vmem = pl.BlockSpec(memory_space=pltpu.VMEM)
    return pl.pallas_call(
        functools.partial(prepare_kernel, first, run),
        out_shape=(
            jax.ShapeDtypeStruct((count * rows, sfts), jnp.bfloat16),
            jax.ShapeDtypeStruct((2, sfts, LANES), jnp.float32),
            jax.ShapeDtypeStruct((3, count * rows, LANES), jnp.float32),
            jax.ShapeDtypeStruct((2 * features, columns), jnp.bfloat16),
        ),
        in_specs=[pl.BlockSpec(memory_space=pltpu.SMEM), vmem, vmem, vmem],
        out_specs=(vmem,) * 4,
        compiler_params=pltpu.CompilerParams(vmem_limit_bytes=16 * 1024 * 1024),
        cost_estimate=pl.CostEstimate(flops=100_000_000, bytes_accessed=4_000_000, transcendentals=0),
        name="prepare",
    )(durations, jnp.broadcast_to(starts[:, None], (rows, LANES)), antenna.T, fractions[None, :])


def statistic_kernel(windows_ref, mask_ref, weigh_ref, coef_ref, kernel_ref, map_ref, loudest_ref):
    values = windows_ref[...].astype(jnp.float32)
    half = LANES // 2
    weighted = (weigh_ref[0] * values + weigh_ref[1] * pltpu.roll(values, half, 1)).astype(jnp.bfloat16)
    templates = map_ref.shape[1]
    rows = map_ref.shape[0] // loudest_ref.shape[1]
    copies = loudest_ref.shape[0]
    per_step = LANES // rows
    for step in range(map_ref.shape[0] // LANES):
        here = pl.ds(step * LANES, LANES)
        sums = jnp.dot(mask_ref[here, :], weighted, preferred_element_type=jnp.float32)
        sums = sums - coef_ref[2, here, :] * pltpu.roll(sums, half, 1)
        parts = jnp.concatenate(split(sums, 2), axis=1)
        found = jnp.dot(parts, kernel_ref[...], preferred_element_type=jnp.float32)
        ra, ia, rb, ib = (found[:, c * templates : (c + 1) * templates] for c in range(4))
        power_a, power_b = ra * ra + ia * ia, rb * rb + ib * ib
        best = None
        for b in range(templates // LANES):
            columns = slice(b * LANES, (b + 1) * LANES)
            result = coef_ref[0, here, :] * power_a[:, columns] + coef_ref[1, here, :] * power_b[:, columns]
            map_ref[here, columns] = result
            best = result if best is None else jnp.maximum(best, result)
        best = jnp.max(jnp.transpose(best), axis=0, keepdims=True)
        for n in range(per_step):
            turned = best if n == 0 else pltpu.roll(best, LANES - n * rows, 1)
            for copy in range(copies):
                loudest_ref[copy, pl.ds(step * per_step + n, 1), :] = turned


def statistic(windows, mask, weigh, coef, kernel, rows, copies):
    count = mask.shape[0] // rows
    templates = kernel.shape[1] // 4
    vmem = pl.BlockSpec(memory_space=pltpu.VMEM)
    return pl.pallas_call(
        statistic_kernel,
        out_shape=(
            jax.ShapeDtypeStruct((count * rows, templates), jnp.float32),
            jax.ShapeDtypeStruct((copies, count, LANES), jnp.float32),
        ),
        in_specs=[vmem] * 5,
        out_specs=(vmem, vmem),
        compiler_params=pltpu.CompilerParams(vmem_limit_bytes=16 * 1024 * 1024),
        cost_estimate=pl.CostEstimate(flops=400_000_000, bytes_accessed=4_000_000, transcendentals=0),
        name="statistic",
    )(windows, mask, weigh, coef, kernel)


def exchange(values, axis, members):
    return lax.all_to_all(values, axis, split_axis=0, concat_axis=0, axis_index_groups=[members], tiled=True)


def body(spectra, offsets, fractions, antenna, starts, durations):
    bands, cores = lax.axis_size("tmpl"), lax.axis_size("tm")
    sft_rows = spectra.shape[0]
    grid_size = starts.shape[0]
    my_rows = grid_size // cores
    me = lax.axis_index("tmpl").astype(jnp.int32)[None]
    by_band = order(bands, bands // 2)
    first = (cores - 1) * bands + bands // 2
    by_run = order(cores * bands, first)
    known = exchange(jnp.broadcast_to(offsets.T[None], (bands,) + offsets.T.shape), "tmpl", by_band)
    my_durations = lax.dynamic_slice_in_dim(durations, lax.axis_index("tm") * my_rows, my_rows, 0)
    windows = pick(me, known, hold(spectra), by_band, [run % bands for run in by_run])
    windows, my_durations = lax.optimization_barrier((windows, my_durations))
    prepared = prepare(my_durations, starts, antenna, fractions, first, sft_rows)
    arrived = exchange(windows.reshape(cores * bands, sft_rows, LANES), ("tm", "tmpl"), by_run)
    fstat_map, loudest = statistic(arrived.reshape(-1, LANES), *prepared, grid_size, bands)
    loudest = jnp.max(exchange(loudest, "tmpl", by_band)[:, :, :grid_size], axis=0)
    return (fstat_map.reshape(my_rows, grid_size, -1), loudest)


def solution(mesh):
    in_specs = (
        P(("grp", "tm", "tmpl"), None, None),
        P(("grp", "tm"), "tmpl"),
        P(("grp", "tmpl")),
        P("grp", None),
        P("grp"),
        P("grp"),
    )
    out_specs = (P("tm", None, ("grp", "tmpl")), P(("grp", "tm"), None))
    return jax.shard_map(body, mesh=mesh, in_specs=in_specs, out_specs=out_specs, check_vma=False)
```

profile of v0, /device:TPU:0, one launch (start us, length us, event | category | flops | bytes accessed | tf_op | source)
XLA Modules:
  0.0 37.4 jit_solution(8216780751246509147)
XLA Ops:
  0.6 1.3 %broadcast_in_dim.9 = s32[8,2,256]{2,1,0:T(2,128)} broadcast(s32[2,256]{1,0:T(2,128)} %bitcast.10), dimensions={1,2} | broadcast | bytes 18432 | tf_op jit(solution)/shard_map/broadcast_in_dim | solution.py:263
  1.9 7.8 %all-to-all-start = ((s32[8,2,256]{2,1,0:T(2,128)}), s32[8,2,256]{2,1,0:T(2,128)S(1)}, u32[]{:S(2)}, u32[]{:S(2)}) async-start(s32[8,2,256]{2,1,0:T(2,128)} %broadcast_in_dim.9), calls=%async_computation | async-start | bytes 32768 | tf_op jit(solution)/shard_map/all_to_all | solution.py:251
  9.8 0.0 copy-start
  9.8 1.6 %copy-done = bf16[32,4,8192]{2,1,0:T(4,128)(2,1)S(1)} copy-done((bf16[32,4,8192]{2,1,0:T(4,128)(2,1)S(1)}, bf16[32,4,8192]{2,1,0:T(4,128)(2,1)}, u32[]{:S(2)}) %copy-start) | copy-done | bytes 2097176
  11.4 0.0 copy-start.4
  11.4 0.1 hold.1.spec_ref
  11.5 0.0 copy-start.3
  11.5 0.0 copy-start.1
  11.5 0.0 copy-start.2
  11.6 0.5 %copy-done.4 = s32[32]{0:T(128)S(1)} copy-done((s32[32]{0:T(128)S(1)}, s32[32]{0:T(128)}, u32[]{:S(2)}) %copy-start.4) | copy-done | bytes 152
  12.0 0.1 dynamic_slice.3.durations_ref
  12.1 1.9 %all-to-all-done.offset_ref = s32[8,2,256]{2,1,0:T(2,128)S(1)} async-done(((s32[8,2,256]{2,1,0:T(2,128)}), s32[8,2,256]{2,1,0:T(2,128)S(1)}, u32[]{:S(2)}, u32[]{:S(2)}) %all-to-all-start) | async-done | bytes 16416 | tf_op jit(solution)/shard_map/all_to_all | solution.py:251
  14.0 2.9 %pick.1 = bf16[512,128]{1,0:T(8,128)(2,1)} custom-call(s32[1]{0:T(128)} %bitcast.me_ref, s32[8,2,256]{2,1,0:T(2,128)S(1)} %all-to-all-done.offset_ref, bf16[32,4,8192]{2,1,0:T(4,128)(2,1)S(1)} %hold.1.spec_ref), custom_call_target="tpu_custom_call" | custom-call | flops 10000000 | bytes 2097152 | tf_op jit(solution)/shard_map/pick/pallas_call | solution.py:110
  16.8 4.0 %all-to-all-start.1 = ((bf16[16,32,128]{2,1,0:T(8,128)(2,1)}), bf16[16,32,128]{2,1,0:T(8,128)(2,1)S(1)}, u32[]{:S(2)}, u32[]{:S(2)}) async-start(bf16[16,32,128]{2,1,0:T(8,128)(2,1)} %bitcast.2), calls=%async_computation.1 | async-start | bytes 262144 | tf_op jit(solution)/shard_map/all_to_all | solution.py:251
  20.8 0.0 copy-done.3
  20.8 0.1 broadcast_in_dim.20.starts_ref
  20.9 0.0 copy-done.1
  20.9 0.0 copy-done.2
  20.9 1.9 %prepare.1 = (bf16[512,512]{1,0:T(8,128)(2,1)S(1)}, f32[2,512,128]{2,1,0:T(8,128)S(1)}, f32[3,512,128]{2,1,0:T(8,128)S(1)}, bf16[256,1024]{1,0:T(8,128)(2,1)S(1)}) custom-call(s32[16]{0:T(128)S(1)} %dynamic_slice.3.durations_ref, s32[32,128]{1,0:T(8,128)S(1)} %broadcast_in_dim.20.starts_ref, f32[4,512]{1,0:T(4,128)S(1)} %bitcast.8, f32[1,256]{1,0:T(1,128)S(1)} %bitcast.9), custom_call_target="tpu_custom_call" | custom-call | flops 100000000 | bytes 4000000 | tf_op jit(solution)/shard_map/prepare/pallas_call | solution.py:187
  22.8 3.3 %all-to-all-done.1 = bf16[16,32,128]{2,1,0:T(8,128)(2,1)S(1)} async-done(((bf16[16,32,128]{2,1,0:T(8,128)(2,1)}), bf16[16,32,128]{2,1,0:T(8,128)(2,1)S(1)}, u32[]{:S(2)}, u32[]{:S(2)}) %all-to-all-start.1) | async-done | bytes 131104 | tf_op jit(solution)/shard_map/all_to_all | solution.py:251
  26.1 2.2 %statistic.1 = (f32[512,256]{1,0:T(8,128)}, f32[8,16,128]{2,1,0:T(8,128)S(1)}) custom-call(bf16[512,128]{1,0:T(8,128)(2,1)S(1)} %bitcast.7, bf16[512,512]{1,0:T(8,128)(2,1)S(1)} %get-tuple-element.12.mask_ref, f32[2,512,128]{2,1,0:T(8,128)S(1)} %get-tuple-element.13.weigh_ref, f32[3,512,128]{2,1,0:T(8,128)S(1)} %get-tuple-element.14.coef_ref, ...), custom_call_target="tpu_custom_call" | custom-call | flops 400000000 | bytes 4000000 | tf_op jit(solution)/shard_map/statistic/pallas_call | solution.py:236
  28.2 8.6 %all_to_all.15 = f32[8,16,128]{2,1,0:T(8,128)S(1)} all-to-all(f32[8,16,128]{2,1,0:T(8,128)S(1)} %get-tuple-element.17), channel_id=1, replica_groups={{8,2,4,6,0,10,12,14},{9,3,5,7,1,11,13,15},{24,18,20,22,16,26,28,30},{25..., dimensions={0} | all-to-all | bytes 131072 | tf_op jit(solution)/shard_map/all_to_all | solution.py:251
  36.8 0.6 %slice_reduce_fusion = f32[16,32]{1,0:T(8,128)} fusion(f32[8,16,128]{2,1,0:T(8,128)S(1)} %all_to_all.15), kind=kLoop, calls=%fused_computation | loop fusion | flops 3584 | bytes 18432 | tf_op jit(solution)/shard_map/reduce_max | solution.py:270
Async XLA Ops:
  1.9 12.0 %all-to-all-start = ((s32[8,2,256]{2,1,0:T(2,128)}), s32[8,2,256]{2,1,0:T(2,128)S(1)}, u32[]{:S(2)}, u32[]{:S(2)}) async-start(s32[8,2,256]{2,1,0:T(2,128)} %broadcast_in_dim.9), calls=%async_computation | async-start | bytes 32768 | tf_op jit(solution)/shard_map/all_to_all | solution.py:251
  9.8 1.6 %copy-start = (bf16[32,4,8192]{2,1,0:T(4,128)(2,1)S(1)}, bf16[32,4,8192]{2,1,0:T(4,128)(2,1)}, u32[]{:S(2)}) copy-start(bf16[32,4,8192]{2,1,0:T(4,128)(2,1)} %spec_ref.1) | copy-start | bytes 6291460
  11.4 0.7 %copy-start.4 = (s32[32]{0:T(128)S(1)}, s32[32]{0:T(128)}, u32[]{:S(2)}) copy-start(s32[32]{0:T(128)} %param.11) | copy-start | bytes 388
  11.5 9.3 %copy-start.3 = (s32[32]{0:T(128)S(1)}, s32[32]{0:T(128)}, u32[]{:S(2)}) copy-start(s32[32]{0:T(128)} %param.10) | copy-start | bytes 388
  11.5 9.4 %copy-start.1 = (f32[512,4]{0,1:T(4,128)S(1)}, f32[512,4]{0,1:T(4,128)}, u32[]{:S(2)}) copy-start(f32[512,4]{0,1:T(4,128)} %param.9) | copy-start | bytes 24580
  11.5 9.3 %copy-start.2 = (f32[256]{0:T(256)S(1)}, f32[256]{0:T(256)}, u32[]{:S(2)}) copy-start(f32[256]{0:T(256)} %param.8) | copy-start | bytes 3076
  16.8 9.3 %all-to-all-start.1 = ((bf16[16,32,128]{2,1,0:T(8,128)(2,1)}), bf16[16,32,128]{2,1,0:T(8,128)(2,1)S(1)}, u32[]{:S(2)}, u32[]{:S(2)}) async-start(bf16[16,32,128]{2,1,0:T(8,128)(2,1)} %bitcast.2), calls=%async_computation.1 | async-start | bytes 262144 | tf_op jit(solution)/shard_map/all_to_all | solution.py:251
where the time goes:
time: 37.8 us; the launch traced here: 37.4 us
  starting transfers between devices  11.8 us (31%)
  blocking collectives  8.59 us (23%)
  Pallas kernels  7.09 us (19%)
  waiting for transfers between devices  5.13 us (14%)
  local copies, waits for them, and re-layouts  3.51 us (9%)
  between operations  0.69 us (2%)
  other arithmetic  0.61 us (2%)
    all_to_all x2, starting transfers between devices, exchange(): lax.all_to_all(values, axis, split_axis=0, concat_axis=0, axis_index_grou...  11.8 us
    all_to_all x1, blocking collectives, exchange(): lax.all_to_all(values, axis, split_axis=0, concat_axis=0, axis_index_grou...  8.59 us
    all_to_all x2, waiting for transfers between devices, exchange(): lax.all_to_all(values, axis, split_axis=0, concat_axis=0, axis_index_grou...  5.13 us
    pallas_call x1, Pallas kernels, pick(): pl.pallas_call(functools.partial(pick_kernel, bands_in, bands_out), out_s...  2.85 us
    pallas_call x1, Pallas kernels, statistic(): pl.pallas_call(statistic_kernel, out_shape=(jax.ShapeDtypeStruct((count *...  2.15 us
    unnamed x10, local copies, waits for them, and re-layouts  2.07 us
    pallas_call x1, Pallas kernels, prepare(): pl.pallas_call(functools.partial(prepare_kernel, first, run), out_shape=(...  1.93 us
    broadcast_in_dim x1, local copies, waits for them, and re-layouts, body(): jnp.broadcast_to(offsets.T[None], (bands,) + offsets.T.shape)  1.29 us
  transfers between devices with their start and end apart: 2, of which 2 were waited for; matrix products, arithmetic and copies ran while one was open for 0% of the time, Pallas kernels for 6%

commit v1 on v0

--- a/solution.py
+++ b/solution.py
@@ -257,8 +257,8 @@
     grid_size = starts.shape[0]
     my_rows = grid_size // cores
     me = lax.axis_index("tmpl").astype(jnp.int32)[None]
-    by_band = order(bands, bands // 2)
-    first = (cores - 1) * bands + bands // 2
+    first = bands // 2 + 1
+    by_band = order(bands, first)
     by_run = order(cores * bands, first)
     known = exchange(jnp.broadcast_to(offsets.T[None], (bands,) + offsets.T.shape), "tmpl", by_band)
     my_durations = lax.dynamic_slice_in_dim(durations, lax.axis_index("tm") * my_rows, my_rows, 0)

time: 37.8 us -> 38.2 us (1.011)
  starting transfers between devices: 11.8 us -> 13.9 us
  waiting for transfers between devices: 5.13 us -> 3.4 us
    all_to_all x2, starting transfers between devices: 11.8 us -> 13.9 us  [exchange(): lax.all_to_all(values, axis, split_axis=0, concat_axis=0, axis_index_grou...]
    all_to_all x2, waiting for transfers between devices: 5.13 us -> 3.4 us  [exchange(): lax.all_to_all(values, axis, split_axis=0, concat_axis=0, axis_index_grou...]
where the time goes in v1:
time: 38.2 us; the launch traced here: 37.8 us
  starting transfers between devices  13.9 us (36%)
  blocking collectives  8.33 us (22%)
  Pallas kernels  7.33 us (19%)
  local copies, waits for them, and re-layouts  3.51 us (9%)
  waiting for transfers between devices  3.4 us (9%)
  between operations  0.69 us (2%)
  other arithmetic  0.61 us (2%)
    all_to_all x2, starting transfers between devices, exchange(): lax.all_to_all(values, axis, split_axis=0, concat_axis=0, axis_index_grou...  13.9 us
    all_to_all x1, blocking collectives, exchange(): lax.all_to_all(values, axis, split_axis=0, concat_axis=0, axis_index_grou...  8.33 us
    all_to_all x2, waiting for transfers between devices, exchange(): lax.all_to_all(values, axis, split_axis=0, concat_axis=0, axis_index_grou...  3.4 us
    pallas_call x1, Pallas kernels, pick(): pl.pallas_call(functools.partial(pick_kernel, bands_in, bands_out), out_s...  2.85 us
    pallas_call x1, Pallas kernels, statistic(): pl.pallas_call(statistic_kernel, out_shape=(jax.ShapeDtypeStruct((count *...  2.17 us
    pallas_call x1, Pallas kernels, prepare(): pl.pallas_call(functools.partial(prepare_kernel, first, run), out_shape=(...  2.17 us
    unnamed x10, local copies, waits for them, and re-layouts  2.07 us
    broadcast_in_dim x1, local copies, waits for them, and re-layouts, body(): jnp.broadcast_to(offsets.T[None], (bands,) + offsets.T.shape)  1.29 us
  transfers between devices with their start and end apart: 2, of which 2 were waited for; matrix products, arithmetic and copies ran while one was open for 0% of the time, Pallas kernels for 6%

profile of v1, /device:TPU:0, one launch (start us, length us, event | category | flops | bytes accessed | tf_op | source)
XLA Modules:
  0.0 37.8 jit_solution(5067814880883680385)
XLA Ops:
  0.6 1.3 %broadcast_in_dim.9 = s32[8,2,256]{2,1,0:T(2,128)} broadcast(s32[2,256]{1,0:T(2,128)} %bitcast.10), dimensions={1,2} | broadcast | bytes 18432 | tf_op jit(solution)/shard_map/broadcast_in_dim | solution.py:263
  1.9 8.3 %all-to-all-start = ((s32[8,2,256]{2,1,0:T(2,128)}), s32[8,2,256]{2,1,0:T(2,128)S(1)}, u32[]{:S(2)}, u32[]{:S(2)}) async-start(s32[8,2,256]{2,1,0:T(2,128)} %broadcast_in_dim.9), calls=%async_computation | async-start | bytes 32768 | tf_op jit(solution)/shard_map/all_to_all | solution.py:251
  10.2 0.0 copy-start
  10.2 1.6 %copy-done = bf16[32,4,8192]{2,1,0:T(4,128)(2,1)S(1)} copy-done((bf16[32,4,8192]{2,1,0:T(4,128)(2,1)S(1)}, bf16[32,4,8192]{2,1,0:T(4,128)(2,1)}, u32[]{:S(2)}) %copy-start) | copy-done | bytes 2097176
  11.8 0.0 copy-start.4
  11.8 0.1 hold.1.spec_ref
  11.9 0.0 copy-start.3
  11.9 0.0 copy-start.1
  12.0 0.0 copy-start.2
  12.0 0.5 %copy-done.4 = s32[32]{0:T(128)S(1)} copy-done((s32[32]{0:T(128)S(1)}, s32[32]{0:T(128)}, u32[]{:S(2)}) %copy-start.4) | copy-done | bytes 152
  12.4 0.1 dynamic_slice.3.durations_ref
  12.5 0.9 %all-to-all-done.offset_ref = s32[8,2,256]{2,1,0:T(2,128)S(1)} async-done(((s32[8,2,256]{2,1,0:T(2,128)}), s32[8,2,256]{2,1,0:T(2,128)S(1)}, u32[]{:S(2)}, u32[]{:S(2)}) %all-to-all-start) | async-done | bytes 16416 | tf_op jit(solution)/shard_map/all_to_all | solution.py:251
  13.4 2.9 %pick.1 = bf16[512,128]{1,0:T(8,128)(2,1)} custom-call(s32[1]{0:T(128)} %bitcast.me_ref, s32[8,2,256]{2,1,0:T(2,128)S(1)} %all-to-all-done.offset_ref, bf16[32,4,8192]{2,1,0:T(4,128)(2,1)S(1)} %hold.1.spec_ref), custom_call_target="tpu_custom_call" | custom-call | flops 10000000 | bytes 2097152 | tf_op jit(solution)/shard_map/pick/pallas_call | solution.py:110
  16.3 5.7 %all-to-all-start.1 = ((bf16[16,32,128]{2,1,0:T(8,128)(2,1)}), bf16[16,32,128]{2,1,0:T(8,128)(2,1)S(1)}, u32[]{:S(2)}, u32[]{:S(2)}) async-start(bf16[16,32,128]{2,1,0:T(8,128)(2,1)} %bitcast.2), calls=%async_computation.1 | async-start | bytes 262144 | tf_op jit(solution)/shard_map/all_to_all | solution.py:251
  22.0 0.0 copy-done.3
  22.0 0.1 broadcast_in_dim.20.starts_ref
  22.1 0.0 copy-done.1
  22.1 0.0 copy-done.2
  22.1 2.2 %prepare.1 = (bf16[512,512]{1,0:T(8,128)(2,1)S(1)}, f32[2,512,128]{2,1,0:T(8,128)S(1)}, f32[3,512,128]{2,1,0:T(8,128)S(1)}, bf16[256,1024]{1,0:T(8,128)(2,1)S(1)}) custom-call(s32[16]{0:T(128)S(1)} %dynamic_slice.3.durations_ref, s32[32,128]{1,0:T(8,128)S(1)} %broadcast_in_dim.20.starts_ref, f32[4,512]{1,0:T(4,128)S(1)} %bitcast.8, f32[1,256]{1,0:T(1,128)S(1)} %bitcast.9), custom_call_target="tpu_custom_call" | custom-call | flops 100000000 | bytes 4000000 | tf_op jit(solution)/shard_map/prepare/pallas_call | solution.py:187
  24.2 2.5 %all-to-all-done.1 = bf16[16,32,128]{2,1,0:T(8,128)(2,1)S(1)} async-done(((bf16[16,32,128]{2,1,0:T(8,128)(2,1)}), bf16[16,32,128]{2,1,0:T(8,128)(2,1)S(1)}, u32[]{:S(2)}, u32[]{:S(2)}) %all-to-all-start.1) | async-done | bytes 131104 | tf_op jit(solution)/shard_map/all_to_all | solution.py:251
  26.7 2.2 %statistic.1 = (f32[512,256]{1,0:T(8,128)}, f32[8,16,128]{2,1,0:T(8,128)S(1)}) custom-call(bf16[512,128]{1,0:T(8,128)(2,1)S(1)} %bitcast.7, bf16[512,512]{1,0:T(8,128)(2,1)S(1)} %get-tuple-element.12.mask_ref, f32[2,512,128]{2,1,0:T(8,128)S(1)} %get-tuple-element.13.weigh_ref, f32[3,512,128]{2,1,0:T(8,128)S(1)} %get-tuple-element.14.coef_ref, ...), custom_call_target="tpu_custom_call" | custom-call | flops 400000000 | bytes 4000000 | tf_op jit(solution)/shard_map/statistic/pallas_call | solution.py:236
  28.9 8.3 %all_to_all.15 = f32[8,16,128]{2,1,0:T(8,128)S(1)} all-to-all(f32[8,16,128]{2,1,0:T(8,128)S(1)} %get-tuple-element.17), channel_id=1, replica_groups={{10,2,4,6,8,0,12,14},{11,3,5,7,9,1,13,15},{26,18,20,22,24,16,28,30},{27..., dimensions={0} | all-to-all | bytes 131072 | tf_op jit(solution)/shard_map/all_to_all | solution.py:251
  37.2 0.6 %slice_reduce_fusion = f32[16,32]{1,0:T(8,128)} fusion(f32[8,16,128]{2,1,0:T(8,128)S(1)} %all_to_all.15), kind=kLoop, calls=%fused_computation | loop fusion | flops 3584 | bytes 18432 | tf_op jit(solution)/shard_map/reduce_max | solution.py:270
Async XLA Ops:
  1.9 11.5 %all-to-all-start = ((s32[8,2,256]{2,1,0:T(2,128)}), s32[8,2,256]{2,1,0:T(2,128)S(1)}, u32[]{:S(2)}, u32[]{:S(2)}) async-start(s32[8,2,256]{2,1,0:T(2,128)} %broadcast_in_dim.9), calls=%async_computation | async-start | bytes 32768 | tf_op jit(solution)/shard_map/all_to_all | solution.py:251
  10.2 1.6 %copy-start = (bf16[32,4,8192]{2,1,0:T(4,128)(2,1)S(1)}, bf16[32,4,8192]{2,1,0:T(4,128)(2,1)}, u32[]{:S(2)}) copy-start(bf16[32,4,8192]{2,1,0:T(4,128)(2,1)} %spec_ref.1) | copy-start | bytes 6291460
  11.8 0.7 %copy-start.4 = (s32[32]{0:T(128)S(1)}, s32[32]{0:T(128)}, u32[]{:S(2)}) copy-start(s32[32]{0:T(128)} %param.11) | copy-start | bytes 388
  11.9 10.1 %copy-start.3 = (s32[32]{0:T(128)S(1)}, s32[32]{0:T(128)}, u32[]{:S(2)}) copy-start(s32[32]{0:T(128)} %param.10) | copy-start | bytes 388
  11.9 10.1 %copy-start.1 = (f32[512,4]{0,1:T(4,128)S(1)}, f32[512,4]{0,1:T(4,128)}, u32[]{:S(2)}) copy-start(f32[512,4]{0,1:T(4,128)} %param.9) | copy-start | bytes 24580
  12.0 10.1 %copy-start.2 = (f32[256]{0:T(256)S(1)}, f32[256]{0:T(256)}, u32[]{:S(2)}) copy-start(f32[256]{0:T(256)} %param.8) | copy-start | bytes 3076
  16.3 10.4 %all-to-all-start.1 = ((bf16[16,32,128]{2,1,0:T(8,128)(2,1)}), bf16[16,32,128]{2,1,0:T(8,128)(2,1)S(1)}, u32[]{:S(2)}, u32[]{:S(2)}) async-start(bf16[16,32,128]{2,1,0:T(8,128)(2,1)} %bitcast.2), calls=%async_computation.1 | async-start | bytes 262144 | tf_op jit(solution)/shard_map/all_to_all | solution.py:251
